TPU v7x, 32 devices: a whole 2x2x4 slice. The times are simulated.
32 devices in a mesh: grp: 2 (over x), ep: 16 (over z, y, core), dp: 1.
Axes of the slice: x: 2, y: 2, z: 4, core: 2. Of those that a mesh axis runs over, the one named last changes fastest.
Arguments:
- rows_in: bfloat16 [2, 256, 4096], P('grp', ('ep', 'dp')), may hold values from -6 to 6
- cotangent: bfloat16 [256, 4096], P(('ep', 'dp')), may hold values from -6 to 6
- lengths: int32 [4], replicated, may hold values from 1 to 128, 256 in all
- train_experts: int32 [256, 8], P(('ep', 'dp')), may hold values from 0 to 15, all different within a row; in each aligned block of 16 rows (0 to 15, 16 to 31, ...) at most 10 rows name the same one
- train_gates: float32 [256, 8], P(('ep', 'dp')), may hold values from 0.02 to 0.3
- decode_experts: int32 [2, 256, 8], P(None, ('ep', 'dp')), may hold values from 0 to 15, all different within a row; in each aligned block of 16 rows (0 to 15, 16 to 31, ..., all dimensions but the last counted through in order) at most 10 rows name the same one
- decode_gates: float32 [2, 256, 8], P(None, ('ep', 'dp')), may hold values from 0.02 to 0.3
- gate_up: bfloat16 [2, 16, 4096, 2, 768], P('grp', 'ep', None, None, 'dp'), may hold values from -0.09375 to 0.09375
- down: bfloat16 [2, 16, 768, 4096], P('grp', 'ep', 'dp'), may hold values from -0.21875 to 0.21875
Outputs:
- result: bfloat16 [2, 256, 4096], P('grp', ('ep', 'dp'))
Inputs may be any that keep to these rules, and one draw needn't show every extreme that they name: `train_experts`: in every aligned block of 16 rows (the rows of one device), the 8 ids of a row differ and no id is named by more than 10 rows of the block; some block reaches 10. `decode_experts`: for each step, in every aligned block of 16 rows (the rows of one device), the 8 ids of a row differ and no id is named by more than 10 rows of the block; some block reaches 10. The lengths sum to 256 and the longest is exactly 128.
All inputs are finite; a program needn't handle non-finite values.
Results may differ from a plain program's by a relative error of at most 0.008.
Values may be sent and summed in bfloat16 or wider, within the bound.
No kernel may reach another device: no remote copies, remote signals or barrier semaphores. Data moves between devices by JAX's collectives and lax.ppermute only.
A program may use at most 192 MiB of HBM per device.

v0:
```python
import jax
import jax.numpy as jnp
from jax import lax
from jax.sharding import PartitionSpec as P

EPSILON = 1e-06


def passed_along(block, axis, distance):
    devices = range(lax.axis_size(axis))
    route = [(i - distance, i) for i in devices if i - distance in devices]
    return lax.ppermute(block, axis, route)


def routing_tables(expert_ids, gate_values, capacity, expert_count):
    row_count, top_count = expert_ids.shape
    flat_ids = expert_ids.reshape(row_count * top_count)
    onehot = (flat_ids[:, None] == jnp.arange(expert_count, dtype=jnp.int32)[None, :]).astype(
        jnp.int32
    )
    earlier = jnp.cumsum(onehot, axis=0) - onehot
    ranks = jnp.sum(earlier * onehot, axis=1)
    slots = flat_ids * capacity + ranks
    hits = (slots[:, None] == jnp.arange(expert_count * capacity, dtype=jnp.int32)[None, :]).astype(
        jnp.float32
    )
    hits = hits.reshape(row_count, top_count, expert_count * capacity)
    picker = jnp.sum(hits, axis=1)
    weigher = jnp.sum(hits * gate_values[:, :, None], axis=1)
    return (picker, weigher)


def replica_sum(per_replica):
    total = jnp.zeros(per_replica.shape[1:], jnp.float32)
    for replica in range(per_replica.shape[0]):
        total = total + lax.optimization_barrier(per_replica[replica].astype(jnp.bfloat16)).astype(
            jnp.float32
        )
    return total


def renew(weights, grads, axis_number, rate):
    scale = jnp.sqrt(jnp.mean(grads * grads, axis=axis_number, keepdims=True) + EPSILON)
    return (weights.astype(jnp.float32) - rate * grads / scale).astype(jnp.bfloat16)


def forward_core(rows_four, weights_gu, weights_dn, part_count):
    ep_count, rep_count, capacity, model_width = rows_four.shape
    hidden_count = weights_gu.shape[2]
    slot_count = ep_count * rep_count * capacity
    both = jnp.dot(
        rows_four.reshape(slot_count, model_width),
        weights_gu.reshape(model_width, 2 * hidden_count),
        preferred_element_type=jnp.float32,
    ).reshape(slot_count, 2, hidden_count)
    active = both[:, 0]
    upward = both[:, 1]
    hidden = (active * jax.nn.sigmoid(active) * upward).astype(jnp.bfloat16)
    piece = jnp.dot(hidden, weights_dn, preferred_element_type=jnp.float32)
    pieces = piece.astype(jnp.bfloat16).reshape(ep_count, rep_count, 1, capacity, model_width)
    return pieces.reshape(ep_count, rep_count * part_count, capacity, model_width)


def learn_core(rows_four, grads_four, weights_gu, weights_dn, part_count):
    ep_count, rep_count, capacity, model_width = rows_four.shape
    hidden_count = weights_gu.shape[2]
    slot_count = ep_count * rep_count * capacity
    flat_grads = grads_four.reshape(slot_count, model_width)
    both = jnp.dot(
        rows_four.reshape(slot_count, model_width),
        weights_gu.reshape(model_width, 2 * hidden_count),
        preferred_element_type=jnp.float32,
    ).reshape(slot_count, 2, hidden_count)
    active = both[:, 0]
    upward = both[:, 1]
    sigma = jax.nn.sigmoid(active)
    swish = active * sigma
    hidden = (swish * upward).astype(jnp.bfloat16)
    back = lax.dot_general(
        flat_grads, weights_dn, (((1,), (1,)), ((), ())), preferred_element_type=jnp.float32
    )
    d_active = back * upward * sigma * (1.0 + active * (1.0 - sigma))
    d_upward = back * swish
    d_both = jnp.stack([d_active, d_upward], axis=1).astype(jnp.bfloat16)
    grad_dn = jnp.einsum(
        "epch,epcd->phd",
        hidden.reshape(ep_count, rep_count, capacity, hidden_count),
        grads_four,
        preferred_element_type=jnp.float32,
    )
    grad_gu = jnp.einsum(
        "epcd,epcgh->pdgh",
        rows_four,
        d_both.reshape(ep_count, rep_count, capacity, 2, hidden_count),
        preferred_element_type=jnp.float32,
    )
    piece = jnp.einsum("mgh,dgh->md", d_both, weights_gu, preferred_element_type=jnp.float32)
    pieces = piece.astype(jnp.bfloat16).reshape(ep_count, rep_count, 1, capacity, model_width)
    ahead = jnp.dot(hidden, weights_dn, preferred_element_type=jnp.float32)
    forward_pieces = ahead.astype(jnp.bfloat16).reshape(
        ep_count, rep_count, 1, capacity, model_width
    )
    slot_dx = pieces.reshape(ep_count, rep_count * part_count, capacity, model_width)
    slot_fw = forward_pieces.reshape(ep_count, rep_count * part_count, capacity, model_width)
    return (grad_gu, grad_dn, slot_dx, slot_fw)


def per_device(
    rows_in,
    cotangent,
    lengths,
    train_experts,
    train_gates,
    decode_experts,
    decode_gates,
    gate_up,
    down,
):
    ep_count = lax.axis_size("ep")
    dp_count = lax.axis_size("dp")
    row_count, model_width = cotangent.shape
    top_count = train_experts.shape[1]
    capacity = min(row_count, max(2, 4 * row_count * top_count // (3 * ep_count)))
    is_learner = lax.axis_index("grp") == 0
    own_gu = gate_up[0, 0]
    own_dn = down[0, 0]
    hidden_all = own_gu.shape[2] * dp_count

    def spread(stacked):
        layers = stacked.shape[0]
        copies = jnp.broadcast_to(
            stacked[:, :, None], (layers, ep_count, dp_count, capacity, model_width)
        )
        copies = copies.reshape(layers, ep_count * dp_count, capacity, model_width)
        arrived = lax.all_to_all(copies, ("ep", "dp"), split_axis=1, concat_axis=1, tiled=True)
        return arrived.reshape(layers, ep_count, dp_count, capacity, model_width)

    def weights_for(weights_gu, weights_dn):
        return (weights_gu, weights_dn, 1)

    def bring_back(slot_out):
        flat_out = slot_out.reshape(ep_count * dp_count, capacity, model_width)
        returned = lax.all_to_all(flat_out, ("ep", "dp"), split_axis=0, concat_axis=0, tiled=True)
        return returned.reshape(ep_count, dp_count, capacity, model_width)

    def combine(mixing, returned):
        total = jnp.sum(returned.astype(jnp.float32), axis=1).reshape(
            ep_count * capacity, model_width
        )
        return jnp.einsum("rs,sd->rd", mixing, total, precision=lax.Precision.HIGHEST)

    def dispatch(picker, values):
        buffer = jnp.einsum(
            "rs,rd->sd", picker.astype(jnp.bfloat16), values, preferred_element_type=jnp.float32
        )
        return buffer.astype(jnp.bfloat16)

    tokens = rows_in[0]
    total_rows = row_count * ep_count * dp_count
    longest = 2 * total_rows // lengths.shape[0]
    first_row = (lax.axis_index("ep") * dp_count + lax.axis_index("dp")) * row_count
    places = first_row + jnp.arange(row_count, dtype=jnp.int32)
    ends = jnp.cumsum(lengths)
    starts = ends - lengths
    inside = (places[:, None] >= starts[None, :]) & (places[:, None] < ends[None, :])
    seq_len = jnp.sum(jnp.where(inside, lengths[None, :], 0), axis=1).astype(jnp.float32)
    weight = 2.0 * longest / (seq_len + longest)
    route_ids = jnp.where(is_learner, train_experts, decode_experts[0])
    route_gates = jnp.where(is_learner, train_gates, decode_gates[0])
    picker, weigher = routing_tables(route_ids, route_gates, capacity, ep_count)
    row_buffer = dispatch(picker, tokens)
    cot_wide = cotangent.astype(jnp.float32)
    grad_buffer = jnp.einsum(
        "rs,rd->sd", weigher * weight[:, None], cot_wide, precision=lax.Precision.HIGHEST
    ).astype(jnp.bfloat16)
    stacked = jnp.stack([row_buffer, grad_buffer], axis=0).reshape(
        2, ep_count, capacity, model_width
    )
    arrived = spread(stacked)
    use_gu, use_dn, part_count = weights_for(own_gu, own_dn)
    per_gu, per_dn, slot_dx, slot_fw = learn_core(
        arrived[0], arrived[1], use_gu, use_dn, part_count
    )
    grad_gu = replica_sum(per_gu)
    grad_dn = replica_sum(per_dn)
    returned = bring_back(jnp.where(is_learner, slot_dx, slot_fw))
    mixing = jnp.where(is_learner, picker, weigher)
    base = jnp.where(is_learner, weight[:, None] * cot_wide, tokens.astype(jnp.float32))
    carried = (base + combine(mixing, returned)).astype(jnp.bfloat16)
    sent_gu = renew(own_gu, grad_gu, 0, 0.5 / model_width**0.5)
    sent_dn = renew(own_dn, grad_dn, 1, 0.5 / hidden_all**0.5)
    fresh_gu, fresh_dn = passed_along((sent_gu, sent_dn), "grp", 1)
    current = carried
    picker, weigher = routing_tables(decode_experts[1], decode_gates[1], capacity, ep_count)
    stacked = dispatch(picker, current).reshape(1, ep_count, capacity, model_width)
    arrived = spread(stacked)
    use_gu, use_dn, part_count = weights_for(fresh_gu, fresh_dn)
    slot_out = forward_core(arrived[0], use_gu, use_dn, part_count)
    returned = bring_back(slot_out)
    current = (current.astype(jnp.float32) + combine(weigher, returned)).astype(jnp.bfloat16)
    final_rows = jnp.where(is_learner, carried, current)
    return final_rows[None]


def solution(mesh):
    placed = (
        P("grp", ("ep", "dp"), None),
        P(("ep", "dp"), None),
        P(),
        P(("ep", "dp"), None),
        P(("ep", "dp"), None),
        P(None, ("ep", "dp"), None),
        P(None, ("ep", "dp"), None),
        P("grp", "ep", None, None, "dp"),
        P("grp", "ep", "dp", None),
    )
    return jax.shard_map(
        per_device,
        mesh=mesh,
        in_specs=placed,
        out_specs=P("grp", ("ep", "dp"), None),
        check_vma=False,
    )
```

profile of v0, /device:TPU:0, one launch (start us, length us, event | category | flops | bytes accessed | tf_op | source)
XLA Modules:
  0.0 624.7 jit_solution(9742883826146676208)
XLA Ops:
  7.5 2.2 convolution_convert_fusion.2
  12.3 2.1 pad_maximum_fusion
  14.4 4.4 copy.86
  18.8 7.6 %all-to-all-start = ((bf16[2,16,10,4096]{3,0,2,1:T(2,128)(2,1)}), bf16[2,16,10,4096]{3,0,2,1:T(2,128)(2,1)S(1)}, u32[]{:S(2)}, u32[]{:S(2)}) async-start(bf16[2,16,10,4096]{3,0,2,1:T(2,128)(2,1)} %copy.86), calls=%async_computation | async-start | bytes 5242880 | tf_op jit(solution)/shard_map/all_to_all | solution.py:135
  26.4 13.1 %copy.105 = bf16[512,8,2,768]{3,1,2,0:T(8,128)(2,1)} copy(bf16[512,8,2,768]{3,2,1,0:T(2,128)(2,1)} %bitcast.131) | data formatting | bytes 25165824
  39.4 16.7 %copy.90 = bf16[1536,4096]{1,0:T(8,128)(2,1)} copy(bf16[1536,4096]{0,1:T(8,128)(2,1)} %bitcast.134) | data formatting | bytes 25165824 | tf_op jit(solution)/shard_map/dot_general | solution.py:69
  56.1 20.4 %all-to-all-done = bf16[2,16,10,4096]{3,0,2,1:T(2,128)(2,1)S(1)} async-done(((bf16[2,16,10,4096]{3,0,2,1:T(2,128)(2,1)}), bf16[2,16,10,4096]{3,0,2,1:T(2,128)(2,1)S(1)}, u32[]{:S(2)}, u32[]{:S(2)}) %all-to-all-start) | async-done | bytes 2621472 | tf_op jit(solution)/shard_map/all_to_all | solution.py:135
  76.6 14.8 %fusion.71 = (bf16[1,16,10,4096]{3,0,2,1:T(2,128)(2,1)}, bf16[16,10,4096]{2,1,0:T(8,128)(2,1)}, bf16[1,16,10,4096]{3,0,2,1:T(2,128)(2,1)}) fusion(bf16[2,16,10,4096]{3,0,2,1:T(2,128)(2,1)S(1)} %all-to-all-done), kind=kLoop, calls=%fused_computation.106 | loop fusion | bytes 6553600 | tf_op jit(solution)/shard_map/slice | solution.py:182
  91.4 2.8 reshape.172
  94.2 3.0 copy.101
  97.1 2.7 reshape_squeeze.10
  99.9 9.0 %fusion.73 = f32[160,2,768]{2,0,1:T(8,128)S(1)} fusion(bf16[160,4096,1]{1,0,2:T(8,128)(2,1)S(1)} %copy-done.1, bf16[2,768,4096]{2,1,0:T(8,128)(2,1)} %bitcast.135), kind=kOutput, calls=%fused_computation.108 | convolution fusion | flops 2013265920 | bytes 14876672 | tf_op jit(solution)/shard_map/dot_general | solution.py:69
  108.9 5.2 fusion.47
  114.4 11.0 %bitcast_convert_fusion = bf16[4096,2,768]{2,0,1:T(8,128)(2,1)} fusion(bf16[1,16,10,4096]{3,0,2,1:T(2,128)(2,1)} %get-tuple-element.9, bf16[16,10,1,768]{3,0,1,2:T(8,128)(2,1)S(1)} %copy.98, bf16[16,10,1,768]{3,0,1,2:T(8,128)(2,1)S(1)} %copy.97), kind=kOutput, calls=%fused_computation.6 | convolution fusion | flops 2020540416 | bytes 14385152 | tf_op jit(solution)/shard_map/epcd,epcgh->pdgh/dot_general | solution.py:91
  125.4 7.1 %fusion.3 = f32[2,768]{1,0:T(2,128)S(1)} fusion(bf16[4096,2,768]{2,0,1:T(8,128)(2,1)} %bitcast_convert_fusion), kind=kLoop, calls=%fused_computation.5 | loop fusion | flops 18872832 | bytes 12589056 | tf_op jit(solution)/shard_map/reduce_sum | solution.py:43
  132.5 15.0 %fusion.2 = bf16[4096,2,768]{2,0,1:T(8,128)(2,1)} fusion(bf16[4096,2,768]{2,0,1:T(8,128)(2,1)} %bitcast_convert_fusion, f32[2,768]{1,0:T(2,128)S(1)} %add_sqrt_fusion, bf16[1,1,4096,2,768]{4,3,2,1,0:T(2,128)(2,1)} %param.16), kind=kLoop, calls=%fused_computation.4 | loop fusion | flops 37748736 | bytes 37754880 | tf_op jit(solution)/shard_map/convert_element_type | solution.py:44
  147.6 7.9 %collective-permute-start = (bf16[4096,2,768]{2,0,1:T(8,128)(2,1)}, bf16[4096,2,768]{2,0,1:T(8,128)(2,1)}, u32[]{:S(2)}, u32[]{:S(2)}) collective-permute-start(bf16[4096,2,768]{2,0,1:T(8,128)(2,1)} %fusion.2), channel_id=1, source_target_pairs={{0,16},{1,17},{2,18},{3,19},{4,20},{5,21},{6,22},{7,23},{8,24},{9,... | collective-permute-start | bytes 37748744 | tf_op jit(solution)/shard_map/ppermute | solution.py:12
  155.7 3.5 bitcast_convert_fusion.1
  160.5 9.2 %fusion.6 = bf16[768,4096]{1,0:T(8,128)(2,1)} fusion(bf16[768,4096]{1,0:T(8,128)(2,1)S(1)} %bitcast_convert_fusion.1, bf16[1,1,768,4096]{3,2,1,0:T(8,128)(2,1)} %param.17, f32[768]{0:T(1024)S(1)} %add_sqrt_fusion.1), kind=kLoop, calls=%fused_computation.11 | loop fusion | flops 18874368 | bytes 18877440 | tf_op jit(solution)/shard_map/convert_element_type | solution.py:44
  169.7 4.0 collective-permute-start.1
  173.7 6.0 fusion.20
  179.7 4.3 fusion.30
  185.6 13.4 %all-to-all-start.1 = ((bf16[16,10,4096]{2,1,0:T(8,128)(2,1)}), bf16[16,10,4096]{2,1,0:T(8,128)(2,1)S(1)}, u32[]{:S(2)}, u32[]{:S(2)}) async-start(bf16[16,10,4096]{2,1,0:T(8,128)(2,1)} %select_n.64), calls=%async_computation.1 | async-start | bytes 4194304 | tf_op jit(solution)/shard_map/all_to_all | solution.py:143
  199.9 40.2 %all-to-all-done.1 = bf16[16,10,4096]{2,1,0:T(8,128)(2,1)S(1)} async-done(((bf16[16,10,4096]{2,1,0:T(8,128)(2,1)}), bf16[16,10,4096]{2,1,0:T(8,128)(2,1)S(1)}, u32[]{:S(2)}, u32[]{:S(2)}) %all-to-all-start.1) | async-done | bytes 1310752 | tf_op jit(solution)/shard_map/all_to_all | solution.py:143
  243.9 58.4 %all_to_all.20 = bf16[1,16,10,4096]{3,2,0,1:T(8,128)(2,1)} all-to-all(bf16[1,16,10,4096]{3,2,0,1:T(8,128)(2,1)S(1)} %bitcast.136), channel_id=1, replica_groups=mesh['grp'=2,'ep'=16,'dp'=1] {'ep','dp'}, dimensions={1} | all-to-all | bytes 2621440 | tf_op jit(solution)/shard_map/all_to_all | solution.py:135
  304.2 117.8 %collective-permute-done = bf16[4096,2,768]{2,0,1:T(8,128)(2,1)} collective-permute-done((bf16[4096,2,768]{2,0,1:T(8,128)(2,1)}, bf16[4096,2,768]{2,0,1:T(8,128)(2,1)}, u32[]{:S(2)}, u32[]{:S(2)}) %collective-permute-start) | collective-permute-done | bytes 12582944 | tf_op jit(solution)/shard_map/ppermute | solution.py:12
  421.9 16.8 %copy.99 = bf16[4096,2,768]{0,2,1:T(8,128)(2,1)} copy(bf16[4096,2,768]{2,0,1:T(8,128)(2,1)} %collective-permute-done) | data formatting | bytes 25165824 | tf_op jit(solution)/shard_map/ppermute | solution.py:12
  438.7 8.9 %fusion.8 = f32[160,2,768]{2,0,1:T(8,128)S(1)} fusion(bf16[160,4096,1]{1,0,2:T(8,128)(2,1)S(1)} %reshape.176, bf16[4096,2,768]{0,2,1:T(8,128)(2,1)} %copy.99), kind=kOutput, calls=%fused_computation.13 | convolution fusion | flops 2013265920 | bytes 14876672 | tf_op jit(solution)/shard_map/dot_general | solution.py:51
  447.6 109.0 %collective-permute-done.1 = bf16[768,4096]{1,0:T(8,128)(2,1)} collective-permute-done((bf16[768,4096]{1,0:T(8,128)(2,1)}, bf16[768,4096]{1,0:T(8,128)(2,1)}, u32[]{:S(2)}, u32[]{:S(2)}) %collective-permute-start.1) | collective-permute-done | bytes 6291488 | tf_op jit(solution)/shard_map/ppermute | solution.py:12
  556.6 4.0 convolution_convert_fusion
  561.1 60.1 %all_to_all.21 = bf16[16,10,4096]{2,1,0:T(8,128)(2,1)} all-to-all(bf16[16,10,4096]{2,1,0:T(8,128)(2,1)S(1)} %reshape_reshape_reshape.3), channel_id=1, replica_groups=mesh['grp'=2,'ep'=16,'dp'=1] {'ep','dp'}, dimensions={0} | all-to-all | bytes 2621440 | tf_op jit(solution)/shard_map/all_to_all | solution.py:143
  621.2 1.8 reshape.171
  (80 shorter events, 21.7 us)
Async XLA Ops:
  3.0 7.2 %copy-start.3 = (bf16[1,16,4096]{2,1,0:T(8,128)(2,1)S(1)}, bf16[1,16,4096]{2,1,0:T(8,128)(2,1)}, u32[]{:S(2)}) copy-start(bf16[1,16,4096]{2,1,0:T(8,128)(2,1)} %param.9) | copy-start | bytes 393220
  6.7 0.6 copy-start.10
  6.8 0.6 copy-start.6
  18.8 57.8 %all-to-all-start = ((bf16[2,16,10,4096]{3,0,2,1:T(2,128)(2,1)}), bf16[2,16,10,4096]{3,0,2,1:T(2,128)(2,1)S(1)}, u32[]{:S(2)}, u32[]{:S(2)}) async-start(bf16[2,16,10,4096]{3,0,2,1:T(2,128)(2,1)} %copy.86), calls=%async_computation | async-start | bytes 5242880 | tf_op jit(solution)/shard_map/all_to_all | solution.py:135
  91.4 2.8 copy-start
  97.1 2.7 copy-start.1
  99.9 9.0 %copy-start.2 = (bf16[160,4096]{1,0:T(8,128)(2,1)S(1)}, bf16[160,4096]{1,0:T(8,128)(2,1)}, u32[]{:S(2)}) copy-start(bf16[160,4096]{1,0:T(8,128)(2,1)} %reshape_squeeze.10) | copy-start | bytes 3932164
  114.0 11.4 %copy-start.4 = (bf16[160,768]{1,0:T(8,128)(2,1)}, bf16[160,768]{1,0:T(8,128)(2,1)S(1)}, u32[]{:S(2)}) copy-start(bf16[160,768]{1,0:T(8,128)(2,1)S(1)} %get-tuple-element.13) | copy-start | bytes 737284
  147.6 274.4 %collective-permute-start = (bf16[4096,2,768]{2,0,1:T(8,128)(2,1)}, bf16[4096,2,768]{2,0,1:T(8,128)(2,1)}, u32[]{:S(2)}, u32[]{:S(2)}) collective-permute-start(bf16[4096,2,768]{2,0,1:T(8,128)(2,1)} %fusion.2), channel_id=1, source_target_pairs={{0,16},{1,17},{2,18},{3,19},{4,20},{5,21},{6,22},{7,23},{8,24},{9,... | collective-permute-start | bytes 37748744 | tf_op jit(solution)/shard_map/ppermute | solution.py:12
  159.2 14.5 %slice-start = ((s8[12582912]{0:T(1024)(128)(4,1)}), s8[4194304]{0:T(1024)(128)(4,1)S(1)}, s32[]{:S(2)}) async-start(s8[12582912]{0:T(1024)(128)(4,1)} %bitcast.132), calls=%async_computation.4 | async-start | bytes 8388608
  160.5 13.2 %slice-start.1 = ((s8[12582912]{0:T(1024)(128)(4,1)}), s8[4194304]{0:T(1024)(128)(4,1)S(1)}, s32[]{:S(2)}) async-start(s8[12582912]{0:T(1024)(128)(4,1)} %bitcast.132), calls=%async_computation.5 | async-start | bytes 8388608
  160.5 13.2 %slice-start.2 = ((s8[12582912]{0:T(1024)(128)(4,1)}), s8[4194304]{0:T(1024)(128)(4,1)S(1)}, s32[]{:S(2)}) async-start(s8[12582912]{0:T(1024)(128)(4,1)} %bitcast.132), calls=%async_computation.6 | async-start | bytes 8388608
  160.5 13.2 %copy-start.5 = (bf16[160,768]{1,0:T(8,128)(2,1)S(1)}, bf16[160,768]{1,0:T(8,128)(2,1)}, u32[]{:S(2)}) copy-start(bf16[160,768]{1,0:T(8,128)(2,1)} %copy-done.4) | copy-start | bytes 737284
  169.7 386.9 %collective-permute-start.1 = (bf16[768,4096]{1,0:T(8,128)(2,1)}, bf16[768,4096]{1,0:T(8,128)(2,1)}, u32[]{:S(2)}, u32[]{:S(2)}) collective-permute-start(bf16[768,4096]{1,0:T(8,128)(2,1)} %fusion.6), channel_id=1, source_target_pairs={{0,16},{1,17},{2,18},{3,19},{4,20},{5,21},{6,22},{7,23},{8,24},{9,... | collective-permute-start | bytes 18874376 | tf_op jit(solution)/shard_map/ppermute | solution.py:12
  185.6 13.5 %copy-start.8 = (s32[16,8]{0,1:T(8,128)S(1)}, s32[16,8]{0,1:T(8,128)}, u32[]{:S(2)}) copy-start(s32[16,8]{0,1:T(8,128)} %get-tuple-element.16) | copy-start | bytes 1540
  185.6 13.5 %copy-start.9 = (f32[2,16,8]{1,2,0:T(8,128)S(1)}, f32[2,16,8]{1,2,0:T(8,128)}, u32[]{:S(2)}) copy-start(f32[2,16,8]{1,2,0:T(8,128)} %param.15) | copy-start | bytes 3076
  185.6 54.6 %all-to-all-start.1 = ((bf16[16,10,4096]{2,1,0:T(8,128)(2,1)}), bf16[16,10,4096]{2,1,0:T(8,128)(2,1)S(1)}, u32[]{:S(2)}, u32[]{:S(2)}) async-start(bf16[16,10,4096]{2,1,0:T(8,128)(2,1)} %select_n.64), calls=%async_computation.1 | async-start | bytes 4194304 | tf_op jit(solution)/shard_map/all_to_all | solution.py:143
  621.2 1.8 copy-start.7
where the time goes:
time: 632 us; the launch traced here: 625 us
  waiting for transfers between devices  287 us (45%)
  blocking collectives  119 us (19%)
  local copies, waits for them, and re-layouts  85.7 us (14%)
  matrix products  58.6 us (9%)
  other arithmetic  40.8 us (6%)
  starting transfers between devices  32.9 us (5%)
    ppermute x2, waiting for transfers between devices, passed_along(): return lax.ppermute(block, axis, route)  227 us
    all_to_all x1, blocking collectives, bring_back(): lax.all_to_all(flat_out, ('ep', 'dp'), split_axis=0, concat_axis=0, tiled...  60.1 us
    all_to_all x1, blocking collectives, spread(): lax.all_to_all(copies, ('ep', 'dp'), split_axis=1, concat_axis=1, tiled=T...  58.4 us
    all_to_all x1, waiting for transfers between devices, bring_back(): lax.all_to_all(flat_out, ('ep', 'dp'), split_axis=0, concat_axis=0, tiled...  40.2 us
    convert_element_type x2, other arithmetic, renew(): (weights.astype(jnp.float32) - rate * grads / scale).astype(jnp.bfloat16)  24.2 us
    all_to_all x1, waiting for transfers between devices, spread(): lax.all_to_all(copies, ('ep', 'dp'), split_axis=1, concat_axis=1, tiled=T...  20.4 us
    ppermute x1, local copies, waits for them, and re-layouts, passed_along(): return lax.ppermute(block, axis, route)  16.8 us
    dot_general x1, local copies, waits for them, and re-layouts, learn_core(): jnp.dot(rows_four.reshape(slot_count, model_width), weights_gu.reshape(mo...  16.7 us
  transfers between devices with their start and end apart: 4, of which 4 were waited for; matrix products, arithmetic and copies ran while one was open for 14% of the time, Pallas kernels for 0%

commit v1 on v0

v1 whole, which is shorter than its diff:
```python
import jax
import jax.numpy as jnp
from jax import lax
from jax.sharding import PartitionSpec as P

EPSILON = 1e-06
AXES = ("ep", "dp")


def across(block, source, target):
    return lax.ppermute(block, "grp", [(source, target)])


def gate_table(expert_ids, gate_values, expert_count):
    named = expert_ids[:, :, None] == jnp.arange(expert_count, dtype=jnp.int32)[None, None, :]
    return jnp.sum(jnp.where(named, gate_values[:, :, None], 0.0), axis=1)


def renew(weights, grads, axis_number, rate):
    scale = jnp.sqrt(jnp.mean(grads * grads, axis=axis_number, keepdims=True) + EPSILON)
    return (weights.astype(jnp.float32) - rate * grads / scale).astype(jnp.bfloat16)


def wide(a, b, contract):
    return lax.dot_general(a, b, (contract, ((), ())), preferred_element_type=jnp.float32)


def expert_ffn(rows, gates, planes, weights_dn):
    active = wide(rows, planes[0], ((1,), (0,)))
    upward = wide(rows, planes[1], ((1,), (0,)))
    hidden = (active * jax.nn.sigmoid(active) * upward).astype(jnp.bfloat16)
    return gates[:, None] * wide(hidden, weights_dn, ((1,), (0,)))


def per_device(
    rows_in,
    cotangent,
    lengths,
    train_experts,
    train_gates,
    decode_experts,
    decode_gates,
    gate_up,
    down,
):
    ep_count = lax.axis_size("ep")
    dp_count = lax.axis_size("dp")
    row_count, model_width = cotangent.shape
    is_learner = lax.axis_index("grp") == 0
    hidden_all = gate_up.shape[4] * dp_count
    own_dn = down[0, 0]
    planes = lax.optimization_barrier(jnp.transpose(gate_up[0, 0], (1, 0, 2)))

    own_rows = rows_in[0]
    total_rows = row_count * ep_count * dp_count
    longest = 2 * total_rows // lengths.shape[0]
    first_row = (lax.axis_index("ep") * dp_count + lax.axis_index("dp")) * row_count
    places = first_row + jnp.arange(row_count, dtype=jnp.int32)
    ends = jnp.cumsum(lengths)
    starts = ends - lengths
    inside = (places[:, None] >= starts[None, :]) & (places[:, None] < ends[None, :])
    seq_len = jnp.sum(jnp.where(inside, lengths[None, :], 0), axis=1).astype(jnp.float32)
    weight = 2.0 * longest / (seq_len + longest)
    cot_wide = weight[:, None] * cotangent.astype(jnp.float32)

    train_table = weight[:, None] * gate_table(train_experts, train_gates, ep_count)
    stale_table = gate_table(decode_experts[0], decode_gates[0], ep_count)
    fresh_table = gate_table(decode_experts[1], decode_gates[1], ep_count)
    table = jnp.concatenate(
        [jnp.where(is_learner, train_table, stale_table), fresh_table], axis=1
    )
    every_table = lax.all_gather(table, AXES, tiled=True)
    mine = lax.axis_index("ep")
    first_gates = lax.dynamic_index_in_dim(every_table, mine, 1, keepdims=False)
    fresh_gates = lax.dynamic_index_in_dim(every_table, mine + ep_count, 1, keepdims=False)

    rows = lax.all_gather(own_rows, AXES, tiled=True)
    cots = lax.all_gather(cotangent, AXES, tiled=True)

    def learn(rows, cots):
        grads = (first_gates[:, None] * cots.astype(jnp.float32)).astype(jnp.bfloat16)
        active = wide(rows, planes[0], ((1,), (0,)))
        upward = wide(rows, planes[1], ((1,), (0,)))
        sigma = jax.nn.sigmoid(active)
        swish = active * sigma
        hidden = (swish * upward).astype(jnp.bfloat16)
        back = wide(grads, own_dn, ((1,), (1,)))
        d_active = (back * upward * sigma * (1.0 + active * (1.0 - sigma))).astype(jnp.bfloat16)
        d_upward = (back * swish).astype(jnp.bfloat16)
        slot_dx = wide(d_active, planes[0], ((1,), (1,))) + wide(d_upward, planes[1], ((1,), (1,)))
        return (slot_dx.astype(jnp.bfloat16), grads, hidden, d_active, d_upward)

    def decode(rows, cots):
        out = expert_ffn(rows, first_gates, planes, own_dn).astype(jnp.bfloat16)
        blank = jnp.zeros((total_rows, own_dn.shape[0]), jnp.bfloat16)
        return (out, cots, blank, blank, blank)

    part, grads, hidden, d_active, d_upward = lax.cond(is_learner, learn, decode, rows, cots)
    summed = lax.psum_scatter(part, AXES, scatter_dimension=0, tiled=True)
    base = jnp.where(is_learner, cot_wide, own_rows.astype(jnp.float32))
    carried = (base + summed.astype(jnp.float32)).astype(jnp.bfloat16)

    def update(rows, grads, hidden, d_active, d_upward):
        rate = 0.5 / model_width**0.5
        fresh_gate = renew(planes[0], wide(rows, d_active, ((0,), (0,))), 0, rate)
        fresh_up = renew(planes[1], wide(rows, d_upward, ((0,), (0,))), 0, rate)
        fresh_dn = renew(own_dn, wide(hidden, grads, ((0,), (0,))), 1, 0.5 / hidden_all**0.5)
        return (jnp.stack([fresh_gate, fresh_up], axis=0), fresh_dn)

    fresh_planes, fresh_dn = lax.cond(
        is_learner,
        update,
        lambda *unused: (planes, own_dn),
        rows,
        grads,
        hidden,
        d_active,
        d_upward,
    )
    arrived = lax.all_gather(across(carried, 1, 0), AXES, tiled=True)
    fresh_part = lax.cond(
        is_learner,
        lambda r: expert_ffn(r, fresh_gates, fresh_planes, fresh_dn).astype(jnp.bfloat16),
        lambda r: r,
        arrived,
    )
    fresh_sum = lax.psum_scatter(fresh_part, AXES, scatter_dimension=0, tiled=True)
    moved = across(fresh_sum, 0, 1)
    final_rows = jnp.where(
        is_learner,
        carried,
        (carried.astype(jnp.float32) + moved.astype(jnp.float32)).astype(jnp.bfloat16),
    )
    return final_rows[None]


def solution(mesh):
    placed = (
        P("grp", ("ep", "dp"), None),
        P(("ep", "dp"), None),
        P(),
        P(("ep", "dp"), None),
        P(("ep", "dp"), None),
        P(None, ("ep", "dp"), None),
        P(None, ("ep", "dp"), None),
        P("grp", "ep", None, None, "dp"),
        P("grp", "ep", "dp", None),
    )
    return jax.shard_map(
        per_device,
        mesh=mesh,
        in_specs=placed,
        out_specs=P("grp", ("ep", "dp"), None),
        check_vma=False,
    )
```

time: 632 us -> 330 us (0.52); the launches traced: 625 us -> 330 us
  waiting for transfers between devices: 287 us -> 178 us
  blocking collectives: 119 us -> 23.6 us
  local copies, waits for them, and re-layouts: 85.7 us -> 23.7 us
  starting transfers between devices: 32.9 us -> 4.82 us
  between operations: 0.8 us -> 13.2 us
  matrix products: 58.6 us -> 50.7 us
    ppermute x2, waiting for transfers between devices: 227 us -> 8.37 us  [across(): return lax.ppermute(block, 'grp', [(source, target)])]
    reduce_scatter x0 -> x2, waiting for transfers between devices: none -> 119 us  [the longest x1 59.9 us: per_device(): lax.psum_scatter(fresh_part, AXES, scatter_dimension=0, tiled=True)]
    all_to_all x2 -> x0, blocking collectives: 119 us -> none  [the longest x1 60.1 us: bring_back(): lax.all_to_all(flat_out, ('ep', 'dp'), split_axis=0, concat_axis=0, tiled...]
    all_to_all x2 -> x0, waiting for transfers between devices: 60.6 us -> none  [the longest x1 40.2 us: bring_back(): lax.all_to_all(flat_out, ('ep', 'dp'), split_axis=0, concat_axis=0, tiled...]
    all_gather x0 -> x3, waiting for transfers between devices: none -> 49.1 us  [the longest x1 42.4 us: per_device(): cots = lax.all_gather(cotangent, AXES, tiled=True)]
    all_gather x0 -> x1, blocking collectives: none -> 23.6 us  [per_device(): every_table = lax.all_gather(table, AXES, tiled=True)]
    another operation x4 -> x3, other arithmetic: 3.3 us -> 26.3 us  [the longest x2 26.1 us: update(): return (jnp.stack([fresh_gate, fresh_up], axis=0), fresh_dn)]
    all_to_all x2 -> x0, starting transfers between devices: 21 us -> none  [the longest x1 13.4 us: bring_back(): lax.all_to_all(flat_out, ('ep', 'dp'), split_axis=0, concat_axis=0, tiled...]
  transfers between devices with their start and end apart: 4 -> 7, of which waited for: 4 -> 6; matrix products, arithmetic and copies ran while one was open for 14% -> 18% of each run, Pallas kernels for 0% -> 0%
where the time goes in v1:
time: 330 us
  waiting for transfers between devices  178 us (54%)
  matrix products  50.7 us (15%)
  other arithmetic  35.5 us (11%)
  local copies, waits for them, and re-layouts  23.7 us (7%)
  blocking collectives  23.6 us (7%)
  between operations  13.2 us (4%)
  starting transfers between devices  4.82 us (1%)
    reduce_scatter x1, waiting for transfers between devices, per_device(): lax.psum_scatter(fresh_part, AXES, scatter_dimension=0, tiled=True)  59.9 us
    reduce_scatter x1, waiting for transfers between devices, per_device(): summed = lax.psum_scatter(part, AXES, scatter_dimension=0, tiled=True)  59.6 us
    dot_general x10, matrix products, wide(): lax.dot_general(a, b, (contract, ((), ())), preferred_element_type=jnp.fl...  50.7 us
    all_gather x1, waiting for transfers between devices, per_device(): cots = lax.all_gather(cotangent, AXES, tiled=True)  42.4 us
    another operation x2, other arithmetic, update(): return (jnp.stack([fresh_gate, fresh_up], axis=0), fresh_dn)  26.1 us
    all_gather x1, blocking collectives, per_device(): every_table = lax.all_gather(table, AXES, tiled=True)  23.6 us
    unnamed x24, local copies, waits for them, and re-layouts  18.9 us
    ppermute x2, waiting for transfers between devices, across(): return lax.ppermute(block, 'grp', [(source, target)])  8.37 us
  transfers between devices with their start and end apart: 7, of which 6 were waited for; matrix products, arithmetic and copies ran while one was open for 18% of the time, Pallas kernels for 0%

profile of v1, /device:TPU:0, one launch (start us, length us, event | category | flops | bytes accessed | tf_op | source)
XLA Modules:
  0.0 329.7 jit_solution(11659596381941689936)
XLA Ops:
  6.6 6.2 %copy.61 = bf16[1,1,768,4096]{3,2,1,0:T(8,128)(2,1)} copy(bf16[1,1,768,4096]{3,2,1,0:T(8,128)(2,1)} %param.23) | data formatting | bytes 12582912
  14.3 11.8 %copy.41 = bf16[1,1,4096,2,768]{4,2,3,1,0:T(8,128)(2,1)} copy(bf16[1,1,4096,2,768]{4,3,2,1,0:T(2,128)(2,1)} %param.22) | data formatting | bytes 25165824 | tf_op args[7]
  26.7 23.6 %all_gather.15 = f32[256,32]{1,0:T(8,128)S(1)} all-gather(f32[16,32]{1,0:T(8,128)S(1)} %pad_maximum_fusion.1), channel_id=1, replica_groups=mesh['grp'=2,'ep'=16,'dp'=1] {'ep','dp'}, dimensions={0}, use_global_device_ids=true | all-gather | bytes 34816 | tf_op jit(solution)/shard_map/all_gather | solution.py:72
  50.5 6.7 %all-gather.9.cloned.1.call-done = bf16[1,256,4096]{2,1,0:T(8,128)(2,1)} async-done(((bf16[1,16,4096]{2,1,0:T(8,128)(2,1)}), bf16[1,256,4096]{2,1,0:T(8,128)(2,1)}) %all-gather.9.cloned.1.call-update) | async-done | bytes 2097168 | tf_op jit(solution)/shard_map/all_gather | solution.py:77
  57.2 42.4 %all-gather.5.cloned.1.call-done = bf16[256,4096]{1,0:T(8,128)(2,1)} async-done(((bf16[16,4096]{1,0:T(8,128)(2,1)}), bf16[256,4096]{1,0:T(8,128)(2,1)}) %all-gather.5.cloned.1.call-update) | async-done | bytes 2097168 | tf_op jit(solution)/shard_map/all_gather | solution.py:78
  99.6 21.5 %conditional.4 = (bf16[256,4096]{1,0:T(8,128)(2,1)}, bf16[256,4096]{1,0:T(8,128)(2,1)}, bf16[256,768]{1,0:T(8,128)(2,1)S(1)}, bf16[256,768]{1,0:T(8,128)(2,1)}, bf16[256,768]{1,0:T(8,128)(2,1)}) conditional(s32[]{:T(128)} %convert_element_type.91, (f32[256]{0:T(256)S(1)}, bf16[2,4096,768]{2,1,0:T(8,128)(2,1)}, bf16[256,4096]{1,0:T(8,128)(2,1)}, ...), branch_computations={%region_5.6_spmd, %region_6.7_spmd} | conditional | flops 8061255680 | bytes 116261984
  99.6 3.6 %multiply_convert_fusion = bf16[256,4096]{1,0:T(8,128)(2,1)} fusion(bf16[256,4096]{1,0:T(8,128)(2,1)} %get-tuple-element.98, f32[256]{0:T(256)S(1)} %get-tuple-element.97), kind=kLoop, calls=%fused_computation.27 | loop fusion | flops 3145728 | bytes 4195328 | tf_op jit(solution)/shard_map/cond/branch_1_fun/convert_element_type | solution.py:81
  103.3 6.0 %fusion.63 = f32[256,768]{1,0:T(8,128)S(1)} fusion(bf16[256,4096]{1,0:T(8,128)(2,1)} %multiply_convert_fusion, bf16[768,4096]{1,0:T(8,128)(2,1)} %get-tuple-element.99), kind=kOutput, calls=%fused_computation.87 | convolution fusion | flops 1610612736 | bytes 9175040 | tf_op jit(solution)/shard_map/cond/branch_1_fun/dot_general | solution.py:25
  109.3 1.8 fusion.21
  111.2 2.9 multiply_convert_fusion.1
  114.1 2.8 fusion.19
  116.9 4.2 %fusion.31 = bf16[256,4096]{1,0:T(8,128)(2,1)} fusion(f32[256,4096]{1,0:T(8,128)S(1)} %fusion.19, bf16[256,768]{1,0:T(8,128)(2,1)} %get-tuple-element.166, bf16[2,4096,768]{2,1,0:T(8,128)(2,1)S(1)} %copy-done), kind=kOutput, calls=%fused_computation.26 | convolution fusion | flops 1612709888 | bytes 12976128 | tf_op jit(solution)/shard_map/cond/branch_1_fun/dot_general | solution.py:25
  121.2 59.6 %reduce-scatter.3.cloned.1.call-done = bf16[16,4096]{1,0:T(8,128)(2,1)} async-done(((bf16[256,4096]{1,0:T(8,128)(2,1)}), bf16[16,4096]{1,0:T(8,128)(2,1)}) %reduce-scatter.3.cloned.1.call-update) | async-done | bytes 131088 | tf_op jit(solution)/shard_map/reduce_scatter | solution.py:99
  180.8 1.0 fusion.60
  181.8 1.3 collective-permute-start
  183.1 5.6 %collective-permute-done = bf16[16,4096]{1,0:T(8,128)(2,1)S(1)} collective-permute-done((bf16[16,4096]{1,0:T(8,128)(2,1)S(1)}, bf16[16,4096]{1,0:T(8,128)(2,1)S(1)}, u32[]{:S(2)}, u32[]{:S(2)}) %collective-permute-start) | collective-permute-done | bytes 131104 | tf_op jit(solution)/shard_map/ppermute | solution.py:11
  189.4 50.2 %conditional.5 = ((bf16[2,4096,768]{2,1,0:T(8,128)(2,1)}, bf16[768,4096]{1,0:T(8,128)(2,1)})) conditional(s32[]{:T(128)} %convert_element_type.91, (bf16[2,4096,768]{2,1,0:T(8,128)(2,1)}, bf16[768,4096]{1,0:T(8,128)(2,1)}) %tuple.73, (bf16[2,4096,768]{2,1,0:T(8,128)(2,1)}, bf16[256,4096]{1,0:T(8,128)(2,1)}, bf16[256,768]{1,0:T(8,128)(2,1)}, ...), branch_computations={%region_8.9_spmd, %region_9.13_spmd} | conditional | flops 4904192512 | bytes 244486400 | solution.py:110
  189.7 8.3 %multiply_reduce_fusion.2 = (f32[768]{0:T(1024)S(1)}, f32[4096,768]{1,0:T(8,128)}) fusion(bf16[256,4096]{1,0:T(8,128)(2,1)} %get-tuple-element.103, bf16[256,768]{1,0:T(8,128)(2,1)} %get-tuple-element.104), kind=kOutput, calls=%fused_computation.41 | convolution fusion | flops 1616903424 | bytes 15076352 | tf_op jit(solution)/shard_map/cond/branch_1_fun/dot_general | solution.py:25
  198.0 7.6 %multiply_reduce_fusion.1 = (f32[768]{0:T(1024)S(1)}, f32[4096,768]{1,0:T(8,128)}) fusion(bf16[256,4096]{1,0:T(8,128)(2,1)S(1)} %copy-done.4, bf16[256,768]{1,0:T(8,128)(2,1)} %get-tuple-element.105), kind=kOutput, calls=%fused_computation.40 | convolution fusion | flops 1616903424 | bytes 15076352 | tf_op jit(solution)/shard_map/cond/branch_1_fun/dot_general | solution.py:25
  205.6 15.1 %fusion.37 = (bf16[1,4096,768]{2,1,0:T(8,128)(2,1)}, bf16[1,4096,768]{2,1,0:T(8,128)(2,1)}) fusion(f32[768]{0:T(1024)S(1)} %get-tuple-element.150, f32[4096,768]{1,0:T(8,128)} %get-tuple-element.144, bf16[2,4096,768]{2,1,0:T(8,128)(2,1)S(1)} %bitcast.99, f32[768]{0:T(1024)S(1)} %get-tuple-element.149, f32[4096,768]{1,0:T(8,128)} %get-tuple-element.146), kind=kLoop, calls=%fused_computation.42 | loop fusion | flops 31457280 | bytes 50337792 | tf_op jit(solution)/shard_map/cond/branch_1_fun/stack | solution.py:108
  220.8 11.0 %pad_maximum_fusion = bf16[2,4096,768]{2,1,0:T(8,128)(2,1)} fusion(bf16[1,4096,768]{2,1,0:T(8,128)(2,1)} %get-tuple-element.142, bf16[1,4096,768]{2,1,0:T(8,128)(2,1)} %get-tuple-element.141), kind=kLoop, calls=%fused_computation.33 | loop fusion | flops 6291456 | bytes 25165824 | tf_op jit(solution)/shard_map/cond/branch_1_fun/stack | solution.py:108
  231.8 1.9 multiply_reduce_fusion
  233.7 3.3 subtract_convert_fusion
  237.0 2.6 copy-done.1
  239.6 16.8 %conditional.6 = (bf16[256,4096]{1,0:T(8,128)(2,1)}) conditional(s32[]{:T(128)} %convert_element_type.91, bf16[256,4096]{1,0:T(8,128)(2,1)} %all-gather.7.cloned.1.call-done, (s32[]{:T(128)}, f32[256,32]{1,0:T(8,128)S(1)}, bf16[2,4096,768]{2,1,0:T(8,128)(2,1)}, bf16[256,4096]{1,0:T(8,128)(2,1)}, bf16[768,4096]{1,0:T(8,128)(2,1)}) %tuple.36), branch_computations={%region_13.14_spmd, %region_14.15_spmd} | conditional | flops 4835115008 | bytes 31001658 | solution.py:121
  239.6 1.6 copy.60
  241.3 4.6 %fusion.41 = f32[256,768]{1,0:T(8,128)S(1)} fusion(bf16[256,4096]{1,0:T(8,128)(2,1)S(1)} %copy.60, bf16[2,4096,768]{2,1,0:T(8,128)(2,1)} %get-tuple-element.112), kind=kOutput, calls=%fused_computation.49 | convolution fusion | flops 1610612736 | bytes 9175040 | tf_op jit(solution)/shard_map/cond/branch_1_fun/dot_general | solution.py:25
  245.9 10.5 %fusion.45 = bf16[256,4096]{1,0:T(8,128)(2,1)} fusion(bf16[768,4096]{1,0:T(8,128)(2,1)} %get-tuple-element.113, f32[256]{0:T(256)S(1)} %bitcast.109, bf16[256,4096]{1,0:T(8,128)(2,1)S(1)} %copy.60, bf16[2,4096,768]{2,1,0:T(8,128)(2,1)} %get-tuple-element.112, f32[256,768]{1,0:T(8,128)S(1)} %fusion.41), kind=kOutput, calls=%fused_computation.54 | convolution fusion | flops 3224502272 | bytes 17564672 | tf_op jit(solution)/shard_map/cond/branch_1_fun/dot_general | solution.py:25
  256.5 59.9 %reduce-scatter.5.cloned.1.call-done = bf16[16,4096]{1,0:T(8,128)(2,1)} async-done(((bf16[256,4096]{1,0:T(8,128)(2,1)}), bf16[16,4096]{1,0:T(8,128)(2,1)}) %reduce-scatter.5.cloned.1.call-update) | async-done | bytes 131088 | tf_op jit(solution)/shard_map/reduce_scatter | solution.py:127
  316.3 3.3 %collective-permute-start.1 = (bf16[16,4096]{1,0:T(8,128)(2,1)}, bf16[16,4096]{1,0:T(8,128)(2,1)S(1)}, u32[]{:S(2)}, u32[]{:S(2)}) collective-permute-start(bf16[16,4096]{1,0:T(8,128)(2,1)} %reduce-scatter.5.cloned.1.call-done), channel_id=1, source_target_pairs={{0,16},{1,17},{2,18},{3,19},{4,20},{5,21},{6,22},{7,23},{8,24},{9,... | collective-permute-start | bytes 393224 | tf_op jit(solution)/shard_map/ppermute | solution.py:11
  319.7 2.8 collective-permute-done.1
  322.5 0.7 fusion.62
  (74 shorter events, 3.1 us)
Async XLA Ops:
  6.5 7.1 %copy-start.15 = (s32[4]{0:T(128)S(1)}, s32[4]{0:T(128)}, u32[]{:S(2)}) copy-start(s32[4]{0:T(128)} %param.17) | copy-start | bytes 52
  6.5 7.3 %copy-start.13 = (s32[16,8]{0,1:T(8,128)S(1)}, s32[16,8]{0,1:T(8,128)}, u32[]{:S(2)}) copy-start(s32[16,8]{0,1:T(8,128)} %param.18) | copy-start | bytes 1540
  6.5 7.4 %copy-start.14 = (f32[16,8]{0,1:T(8,128)S(1)}, f32[16,8]{0,1:T(8,128)}, u32[]{:S(2)}) copy-start(f32[16,8]{0,1:T(8,128)} %param.19) | copy-start | bytes 1540
  6.5 7.4 %copy-start.11 = (s32[2,16,8]{1,2,0:T(8,128)S(1)}, s32[2,16,8]{1,2,0:T(8,128)}, u32[]{:S(2)}) copy-start(s32[2,16,8]{1,2,0:T(8,128)} %param.20) | copy-start | bytes 3076
  6.5 7.6 %copy-start.12 = (f32[2,16,8]{1,2,0:T(8,128)S(1)}, f32[2,16,8]{1,2,0:T(8,128)}, u32[]{:S(2)}) copy-start(f32[2,16,8]{1,2,0:T(8,128)} %param.21) | copy-start | bytes 3076
  6.5 50.6 %all-gather.9.cloned.1.call-start = ((), (), s32[]{:S(2)}) async-start(), calls=%async_computation.6 | async-start | bytes 2228224 | tf_op jit(solution)/shard_map/all_gather | solution.py:77
  12.8 86.8 %all-gather.5.cloned.1.call-start = ((), (), s32[]{:S(2)}) async-start(), calls=%async_computation.2 | async-start | bytes 2228224 | tf_op jit(solution)/shard_map/all_gather | solution.py:78
  13.6 167.2 %reduce-scatter.3.cloned.1.call-start = ((), (), s32[]{:S(2)}) async-start(), calls=%async_computation.3 | async-start | bytes 2228224 | tf_op jit(solution)/shard_map/reduce_scatter | solution.py:99
  99.6 81.1 %copy-start.6 = (bf16[1,16,4096]{2,1,0:T(8,128)(2,1)S(1)}, bf16[1,16,4096]{2,1,0:T(8,128)(2,1)}, u32[]{:S(2)}) copy-start(bf16[1,16,4096]{2,1,0:T(8,128)(2,1)} %param.15) | copy-start | bytes 393220
  99.6 81.1 %copy-start.7 = (bf16[16,4096]{1,0:T(8,128)(2,1)S(1)}, bf16[16,4096]{1,0:T(8,128)(2,1)}, u32[]{:S(2)}) copy-start(bf16[16,4096]{1,0:T(8,128)(2,1)} %param.16) | copy-start | bytes 393220
  99.6 9.7 %copy-start = (bf16[2,4096,768]{2,1,0:T(8,128)(2,1)S(1)}, bf16[2,4096,768]{2,1,0:T(8,128)(2,1)}, u32[]{:S(2)}) copy-start(bf16[2,4096,768]{2,1,0:T(8,128)(2,1)} %get-tuple-element.101) | copy-start | bytes 37748740 | tf_op jit(solution)/shard_map/conditional
  103.3 6.1 %copy-start.3 = (bf16[256,4096]{1,0:T(8,128)(2,1)S(1)}, bf16[256,4096]{1,0:T(8,128)(2,1)}, u32[]{:S(2)}) copy-start(bf16[256,4096]{1,0:T(8,128)(2,1)} %get-tuple-element.100) | copy-start | bytes 6291460 | tf_op jit(solution)/shard_map/conditional
  121.1 118.5 %all-gather.7.cloned.1.call-start = ((), (), s32[]{:S(2)}) async-start(), calls=%async_computation.4 | async-start | bytes 2228224 | tf_op jit(solution)/shard_map/all_gather | solution.py:120
  181.8 7.6 %copy-start.8 = (bf16[16,4096]{1,0:T(8,128)(2,1)}, bf16[16,4096]{1,0:T(8,128)(2,1)S(1)}, u32[]{:S(2)}) copy-start(bf16[16,4096]{1,0:T(8,128)(2,1)S(1)} %fusion.60) | copy-start | bytes 393220
  181.8 6.9 %collective-permute-start = (bf16[16,4096]{1,0:T(8,128)(2,1)S(1)}, bf16[16,4096]{1,0:T(8,128)(2,1)S(1)}, u32[]{:S(2)}, u32[]{:S(2)}) collective-permute-start(bf16[16,4096]{1,0:T(8,128)(2,1)S(1)} %fusion.60), channel_id=1, source_target_pairs={{16,0},{17,1},{18,2},{19,3},{20,4},{21,5},{22,6},{23,7},{24,8},{25... | collective-permute-start | bytes 393224 | tf_op jit(solution)/shard_map/ppermute | solution.py:11
  188.7 0.6 copy-start.10
  189.3 127.0 %reduce-scatter.5.cloned.1.call-start = ((), (), s32[]{:S(2)}) async-start(), calls=%async_computation.5 | async-start | bytes 2228224 | tf_op jit(solution)/shard_map/reduce_scatter | solution.py:127
  189.6 8.3 %copy-start.4 = (bf16[256,4096]{1,0:T(8,128)(2,1)S(1)}, bf16[256,4096]{1,0:T(8,128)(2,1)}, u32[]{:S(2)}) copy-start(bf16[256,4096]{1,0:T(8,128)(2,1)} %get-tuple-element.103) | copy-start | bytes 6291460 | tf_op jit(solution)/shard_map/cond
  189.6 15.9 %slice-start = ((s8[12582912]{0:T(1024)(128)(4,1)}), s8[4194304]{0:T(1024)(128)(4,1)S(1)}, s32[]{:S(2)}) async-start(s8[12582912]{0:T(1024)(128)(4,1)} %bitcast.98), calls=%async_computation.7 | async-start | bytes 8388608 | tf_op jit(solution)/shard_map/cond
  189.7 15.9 %slice-start.1 = ((s8[12582912]{0:T(1024)(128)(4,1)}), s8[4194304]{0:T(1024)(128)(4,1)S(1)}, s32[]{:S(2)}) async-start(s8[12582912]{0:T(1024)(128)(4,1)} %bitcast.98), calls=%async_computation.8 | async-start | bytes 8388608 | tf_op jit(solution)/shard_map/cond
  198.0 7.6 %slice-start.2 = ((s8[12582912]{0:T(1024)(128)(4,1)}), s8[4194304]{0:T(1024)(128)(4,1)S(1)}, s32[]{:S(2)}) async-start(s8[12582912]{0:T(1024)(128)(4,1)} %bitcast.98), calls=%async_computation.9 | async-start | bytes 8388608 | tf_op jit(solution)/shard_map/cond
  198.0 35.7 %slice-start.3 = ((s8[6291456]{0:T(1024)(128)(4,1)}), s8[4194304]{0:T(1024)(128)(4,1)S(1)}, s32[]{:S(2)}) async-start(s8[6291456]{0:T(1024)(128)(4,1)} %bitcast.104), calls=%async_computation.10 | async-start | bytes 8388608 | tf_op jit(solution)/shard_map/cond
  205.6 28.1 %slice-start.4 = ((s8[6291456]{0:T(1024)(128)(4,1)}), s8[2097152]{0:T(1024)(128)(4,1)S(1)}, s32[]{:S(2)}) async-start(s8[6291456]{0:T(1024)(128)(4,1)} %bitcast.104), calls=%async_computation.11 | async-start | bytes 4194304 | tf_op jit(solution)/shard_map/cond
  220.8 11.0 %copy-start.5 = (bf16[256,4096]{1,0:T(8,128)(2,1)S(1)}, bf16[256,4096]{1,0:T(8,128)(2,1)}, u32[]{:S(2)}) copy-start(bf16[256,4096]{1,0:T(8,128)(2,1)} %get-tuple-element.108) | copy-start | bytes 6291460 | tf_op jit(solution)/shard_map/cond
  237.0 2.6 copy-start.1
  239.6 82.9 %copy-start.9 = (bf16[16,4096]{1,0:T(8,128)(2,1)S(1)}, bf16[16,4096]{1,0:T(8,128)(2,1)}, u32[]{:S(2)}) copy-start(bf16[16,4096]{1,0:T(8,128)(2,1)} %copy-done.8) | copy-start | bytes 393220
  316.3 6.1 %collective-permute-start.1 = (bf16[16,4096]{1,0:T(8,128)(2,1)}, bf16[16,4096]{1,0:T(8,128)(2,1)S(1)}, u32[]{:S(2)}, u32[]{:S(2)}) collective-permute-start(bf16[16,4096]{1,0:T(8,128)(2,1)} %reduce-scatter.5.cloned.1.call-done), channel_id=1, source_target_pairs={{0,16},{1,17},{2,18},{3,19},{4,20},{5,21},{6,22},{7,23},{8,24},{9,... | collective-permute-start | bytes 393224 | tf_op jit(solution)/shard_map/ppermute | solution.py:11
Sparse Core Ops, SparseCore 0:
  13.0 44.1 all-gather.8
  59.3 40.2 all-gather.4
  121.3 59.4 reduce-scatter.2
  189.5 39.4 all-gather.6
  256.6 59.7 reduce-scatter.4
